TPU v7x, 32 devices: a whole 2x2x4 slice. The times are simulated.
32 devices in a mesh: dp: 16 (over z, y, core), seq: 2 (over x).
Axes of the slice: x: 2, y: 2, z: 4, core: 2. Of those that a mesh axis runs over, the one named last changes fastest.
Arguments:
- tile_feats: bfloat16 [8192, 2048], P('dp'), may hold values from -6 to 6
- tile_pos: int32 [16, 512], P('dp'), may hold values from -1 to 511, as said below
- slide_count: int32 [16], P('dp'), may hold values from 128 to 512, as said below
- w_proj: bfloat16 [2048, 768], P(None, 'seq'), may hold values from -0.125 to 0.125
- emb_grad: bfloat16 [16, 512, 768], P('dp', 'seq'), may hold values from -6 to 6
- ln_gain: float32 [768], replicated, may hold values from 0.25 to 1.75
- w_qkv: bfloat16 [768, 2304], P('dp'), may hold values from -1.5 to 1.5
- w_out: bfloat16 [768, 768], P('dp'), may hold values from -0.21875 to 0.21875
Outputs:
- slide_emb: bfloat16 [16, 512, 768], P('dp', 'seq')
- attn_branch: bfloat16 [16, 512, 768], P('dp', 'seq')
- proj_grad: float32 [2048, 768], P(None, 'seq')
Inputs may be any that keep to these rules, and one draw needn't show every extreme that they name: `tile_pos`: slot j of a row belongs to slide j // 32. Each position below a slide's slide_count is held by exactly one slot of that slide over all rows; all other slots hold -1. `slide_count`: some slide is full.
All inputs are finite; a program needn't handle non-finite values.
Results may differ from a plain program's by a relative error of at most 0.017.
The roundings to bfloat16 on the way count: a program that leaves them out, or rounds other values in their place, can miss the bound.
Values may be sent and summed in bfloat16 or wider, within the bound.
A program may use at most 128 MiB of HBM per device.

v0:
```python
import jax
import jax.numpy as jnp
from jax import lax
from jax.sharding import PartitionSpec as P

D = 768
HEAD_COUNT = 12
HEAD_WIDTH = 64
DILATION_STEP = 4
NEGATIVE = -1e30
EPSILON = 1e-05


def selection_shift(values, heads, dilation):
    length = values.shape[1]
    rest = values.shape[2:]
    shaped = values.reshape((heads, length // dilation, dilation) + rest)
    return jnp.stack(
        [shaped[head_number, :, head_number % dilation] for head_number in range(heads)]
    )


def insertion_shift(values, chosen, heads, dilation):
    length = values.shape[1]
    rest = values.shape[2:]
    shaped = values.reshape((heads, length // dilation, dilation) + rest)
    shift_amounts = jnp.arange(heads, dtype=jnp.int32) % dilation
    select = jnp.arange(dilation, dtype=jnp.int32)[None, :] == shift_amounts[:, None]
    select = select.reshape((heads, 1, dilation) + (1,) * len(rest))
    merged = jnp.where(select, chosen[:, :, None], shaped)
    return merged.reshape(values.shape)


def local(tile_feats, tile_pos, slide_count, w_proj, emb_grad, ln_gain, w_qkv, w_out):
    seq_count = lax.axis_size("seq")
    seq_index = lax.axis_index("seq")
    slot_rows = tile_feats.shape[0]
    nearby_length = emb_grad.shape[1]
    slide_len = nearby_length * seq_count
    inner = HEAD_COUNT * HEAD_WIDTH
    scale = HEAD_WIDTH ** (-0.5)
    tile_count = slide_count[0]
    emb_part = jnp.dot(tile_feats, w_proj, preferred_element_type=jnp.float32).astype(jnp.bfloat16)
    feature_part = emb_part.shape[1]
    positions = tile_pos.reshape(slot_rows)
    arrived, arrived_pos = (
        lax.all_to_all(emb_part, "dp", split_axis=0, concat_axis=0, tiled=True),
        lax.all_to_all(positions, "dp", split_axis=0, concat_axis=0, tiled=True),
    )
    target = jnp.where(arrived_pos >= 0, arrived_pos, slide_len).astype(jnp.int32)
    slide_rows = (
        jnp.zeros((slide_len + 1, feature_part), jnp.bfloat16).at[target].set(arrived)[:slide_len]
    )
    local_emb = lax.all_to_all(slide_rows, "seq", split_axis=0, concat_axis=1, tiled=True)
    widened = local_emb.astype(jnp.float32)
    center = jnp.mean(widened, axis=-1, keepdims=True)
    spread = jnp.mean(jnp.square(widened - center), axis=-1, keepdims=True)
    normed = ((widened - center) * lax.rsqrt(spread + EPSILON) * ln_gain).astype(jnp.bfloat16)
    columns = normed
    projected = jnp.dot(
        columns, lax.all_gather(w_qkv, "dp", axis=0, tiled=True), preferred_element_type=jnp.float32
    )
    projected = projected.astype(jnp.bfloat16)
    query_rows = projected[:, :inner].reshape(nearby_length, HEAD_COUNT, HEAD_WIDTH)
    key_matrix = projected[:, inner : 2 * inner].reshape(nearby_length, HEAD_COUNT, HEAD_WIDTH)
    value_matrix = projected[:, 2 * inner :].reshape(nearby_length, HEAD_COUNT, HEAD_WIDTH)
    sequence_position = seq_index * nearby_length + jnp.arange(nearby_length, dtype=jnp.int32)
    occupied = sequence_position < tile_count
    shift_amounts = jnp.arange(HEAD_COUNT, dtype=jnp.int32) % DILATION_STEP
    local_scores = (
        jnp.einsum("qhd,khd->hqk", query_rows, key_matrix, preferred_element_type=jnp.float32)
        * scale
    )
    local_ok = jnp.broadcast_to(occupied[None, None, :], local_scores.shape)
    nearby_maximum = jnp.max(jnp.where(local_ok, local_scores, NEGATIVE), axis=-1)
    local_weight = jnp.where(local_ok, jnp.exp(local_scores - nearby_maximum[..., None]), 0.0)
    nearby_sum = jnp.sum(local_weight, axis=-1)
    nearby_accumulator = jnp.einsum("hqk,khd->hqd", local_weight, value_matrix.astype(jnp.float32))
    stepped_queries = query_rows.reshape(
        nearby_length // DILATION_STEP, DILATION_STEP, HEAD_COUNT, HEAD_WIDTH
    )
    selected_query = jnp.stack(
        [
            stepped_queries[:, head_number % DILATION_STEP, head_number, :]
            for head_number in range(HEAD_COUNT)
        ]
    )
    key_value = jnp.concatenate([key_matrix, value_matrix], axis=-1)
    flat_rows = key_value.reshape(nearby_length, HEAD_COUNT * 2 * HEAD_WIDTH)
    portion = lax.all_gather(flat_rows, "seq", axis=0, tiled=True)
    row_counts = portion.shape[0]
    head_split = (row_counts + DILATION_STEP - 1) // DILATION_STEP
    shaped = portion.reshape(row_counts, HEAD_COUNT, 2 * HEAD_WIDTH)
    leading_index = shift_amounts % DILATION_STEP
    index_of_row = (
        leading_index[:, None] + DILATION_STEP * jnp.arange(head_split, dtype=jnp.int32)[None, :]
    )
    inside = index_of_row < row_counts
    safe_index = jnp.minimum(index_of_row, row_counts - 1)
    head_index = jnp.arange(HEAD_COUNT, dtype=jnp.int32)[:, None]
    chosen = shaped[safe_index, head_index, :]
    key_ok = inside & (index_of_row < tile_count)
    previous_maximum = selection_shift(nearby_maximum, HEAD_COUNT, DILATION_STEP)
    previous_sum = selection_shift(nearby_sum, HEAD_COUNT, DILATION_STEP)
    previous_accumulator = selection_shift(nearby_accumulator, HEAD_COUNT, DILATION_STEP)
    far_scores = (
        jnp.einsum(
            "hqd,hkd->hqk",
            selected_query,
            chosen[..., :HEAD_WIDTH],
            preferred_element_type=jnp.float32,
        )
        * scale
    )
    usable = jnp.broadcast_to(key_ok[:, None, :], far_scores.shape)
    new_max = jnp.maximum(
        previous_maximum, jnp.max(jnp.where(usable, far_scores, NEGATIVE), axis=-1)
    )
    far_weight = jnp.where(usable, jnp.exp(far_scores - new_max[..., None]), 0.0)
    rescale = jnp.exp(previous_maximum - new_max)
    updated_sum = previous_sum * rescale + jnp.sum(far_weight, axis=-1)
    updated_accumulator = previous_accumulator * rescale[..., None] + jnp.einsum(
        "hqk,hkd->hqd", far_weight, chosen[..., HEAD_WIDTH:].astype(jnp.float32)
    )
    complete_sum = insertion_shift(nearby_sum, updated_sum, HEAD_COUNT, DILATION_STEP)
    complete_accumulator = insertion_shift(
        nearby_accumulator, updated_accumulator, HEAD_COUNT, DILATION_STEP
    )
    safe_total = jnp.where(occupied[None, :], complete_sum, 1.0)
    context = jnp.where(occupied[None, :, None], complete_accumulator / safe_total[..., None], 0.0)
    context = context.transpose(1, 0, 2).reshape(nearby_length, inner).astype(jnp.bfloat16)
    columns = context
    branch_out = jnp.dot(
        columns, lax.all_gather(w_out, "dp", axis=0, tiled=True), preferred_element_type=jnp.float32
    )
    attn_branch = branch_out.astype(jnp.bfloat16)
    returned_grad = lax.all_to_all(
        emb_grad.reshape(nearby_length, D), "seq", split_axis=1, concat_axis=0, tiled=True
    )
    padded_grad = jnp.concatenate(
        [returned_grad, jnp.zeros((1, feature_part), jnp.bfloat16)], axis=0
    )
    picked_grad = padded_grad[target]
    slot_grad = lax.all_to_all(picked_grad, "dp", split_axis=0, concat_axis=0, tiled=True)
    grad_part = lax.dot_general(
        tile_feats, slot_grad, (((0,), (0,)), ((), ())), preferred_element_type=jnp.float32
    )
    proj_grad = lax.psum(grad_part, "dp")
    return (local_emb[None], attn_branch[None], proj_grad)


def solution(mesh):
    in_specs = (
        P("dp", None),
        P("dp", None),
        P("dp"),
        P(None, "seq"),
        P("dp", "seq", None),
        P(),
        P("dp", None),
        P("dp", None),
    )
    out_specs = (P("dp", "seq", None), P("dp", "seq", None), P(None, "seq"))
    return jax.shard_map(local, mesh=mesh, in_specs=in_specs, out_specs=out_specs, check_vma=False)
```

profile of v0, /device:TPU:0, one launch (start us, length us, event | category | flops | bytes accessed | tf_op | source)
XLA Modules:
  0.0 267.3 jit_solution(15064173347911541342)
XLA Ops:
  7.2 0.7 all-gather.4.cloned.1.call-update
  8.4 1.3 reduce.56
  9.8 0.7 all_to_all.50
  10.5 7.4 %all-to-all-start = ((s32[16,32,1]{1,2,0:T(1,128)}), s32[16,32,1]{1,2,0:T(1,128)S(1)}, u32[]{:S(2)}, u32[]{:S(2)}) async-start(s32[16,32,1]{1,2,0:T(1,128)} %all_to_all.50), calls=%async_computation | async-start | bytes 16384 | tf_op jit(solution)/shard_map/all_to_all | solution.py:48
  17.9 3.5 %convolution_convert_fusion.2 = bf16[512,384]{1,0:T(8,128)(2,1)} fusion(bf16[512,2048]{1,0:T(8,128)(2,1)S(1)} %copy-done, bf16[2048,384]{1,0:T(8,128)(2,1)} %param.11), kind=kOutput, calls=%fused_computation.14 | convolution fusion | flops 805502976 | bytes 4063232 | tf_op jit(solution)/shard_map/dot_general | solution.py:43
  21.3 2.9 %all-to-all-done = s32[16,32,1]{1,2,0:T(1,128)S(1)} async-done(((s32[16,32,1]{1,2,0:T(1,128)}), s32[16,32,1]{1,2,0:T(1,128)S(1)}, u32[]{:S(2)}, u32[]{:S(2)}) %all-to-all-start) | async-done | bytes 2080 | tf_op jit(solution)/shard_map/all_to_all | solution.py:48
  24.2 3.6 %all-to-all-start.1 = ((bf16[16,32,384]{2,1,0:T(8,128)(2,1)}), bf16[16,32,384]{2,1,0:T(8,128)(2,1)S(1)}, u32[]{:S(2)}, u32[]{:S(2)}) async-start(bf16[16,32,384]{2,1,0:T(8,128)(2,1)} %bitcast.1), calls=%async_computation.1 | async-start | bytes 786432 | tf_op jit(solution)/shard_map/all_to_all | solution.py:47
  27.9 0.8 copy.164
  28.6 0.7 reduce.57
  29.4 12.1 %all-to-all-done.1 = bf16[16,32,384]{2,1,0:T(8,128)(2,1)S(1)} async-done(((bf16[16,32,384]{2,1,0:T(8,128)(2,1)}), bf16[16,32,384]{2,1,0:T(8,128)(2,1)S(1)}, u32[]{:S(2)}, u32[]{:S(2)}) %all-to-all-start.1) | async-done | bytes 393248 | tf_op jit(solution)/shard_map/all_to_all | solution.py:47
  41.5 0.7 copy-done.3
  42.2 3.5 %all-to-all-start.3 = ((bf16[256,2,384]{2,0,1:T(8,128)(2,1)}), bf16[256,2,384]{2,0,1:T(8,128)(2,1)S(1)}, u32[]{:S(2)}, u32[]{:S(2)}) async-start(bf16[256,2,384]{2,0,1:T(8,128)(2,1)} %copy.164), calls=%async_computation.3 | async-start | bytes 786432 | tf_op jit(solution)/shard_map/all_to_all | solution.py:137
  45.7 2.9 %scatter_custom_fusion = bf16[513,384]{1,0:T(8,128)(2,1)S(1)} fusion(s32[512]{0:T(512)S(1)} %bitcast.199, bf16[512,384]{1,0:T(8,128)(2,1)} %bitcast.185, bf16[]{:T(256)} %constant.24.clone.1), kind=kCustom, calls=%fused_computation.31 | custom fusion | bytes 394496 | tf_op jit(solution)/shard_map/scatter | solution.py:52
  48.6 0.8 slice.220
  49.4 3.2 %all-to-all-done.3 = bf16[256,2,384]{2,0,1:T(8,128)(2,1)S(1)} async-done(((bf16[256,2,384]{2,0,1:T(8,128)(2,1)}), bf16[256,2,384]{2,0,1:T(8,128)(2,1)S(1)}, u32[]{:S(2)}, u32[]{:S(2)}) %all-to-all-start.3) | async-done | bytes 393248 | tf_op jit(solution)/shard_map/all_to_all | solution.py:137
  52.6 3.5 %all-to-all-start.2 = ((bf16[2,256,384]{2,1,0:T(8,128)(2,1)}), bf16[2,256,384]{2,1,0:T(8,128)(2,1)S(1)}, u32[]{:S(2)}, u32[]{:S(2)}) async-start(bf16[2,256,384]{2,1,0:T(8,128)(2,1)} %bitcast.3), calls=%async_computation.2 | async-start | bytes 786432 | tf_op jit(solution)/shard_map/all_to_all | solution.py:54
  56.1 2.6 gather_fusion.1
  58.7 3.5 %all-to-all-done.2 = bf16[2,256,384]{2,1,0:T(8,128)(2,1)S(1)} async-done(((bf16[2,256,384]{2,1,0:T(8,128)(2,1)}), bf16[2,256,384]{2,1,0:T(8,128)(2,1)S(1)}, u32[]{:S(2)}, u32[]{:S(2)}) %all-to-all-start.2) | async-done | bytes 393248 | tf_op jit(solution)/shard_map/all_to_all | solution.py:54
  62.1 4.8 %all-to-all-start.4 = ((bf16[16,32,384]{2,1,0:T(8,128)(2,1)}), bf16[16,32,384]{2,1,0:T(8,128)(2,1)}, u32[]{:S(2)}, u32[]{:S(2)}) async-start(bf16[16,32,384]{2,1,0:T(8,128)(2,1)} %bitcast.50), calls=%async_computation.4 | async-start | bytes 786432 | tf_op jit(solution)/shard_map/all_to_all | solution.py:144
  67.0 0.9 bitcast_convert_fusion
  67.9 1.4 copy.125
  69.3 9.9 %all-to-all-done.4 = bf16[16,32,384]{2,1,0:T(8,128)(2,1)} async-done(((bf16[16,32,384]{2,1,0:T(8,128)(2,1)}), bf16[16,32,384]{2,1,0:T(8,128)(2,1)}, u32[]{:S(2)}, u32[]{:S(2)}) %all-to-all-start.4) | async-done | bytes 393248 | tf_op jit(solution)/shard_map/all_to_all | solution.py:144
  79.2 3.7 %convolution_bitcast_fusion = f32[2048,384]{0,1:T(8,128)} fusion(bf16[512,384]{1,0:T(8,128)(2,1)} %bitcast.51, bf16[512,2048]{1,0:T(8,128)(2,1)S(1)} %copy-done), kind=kOutput, calls=%fused_computation.6 | convolution fusion | flops 805306368 | bytes 5636096 | tf_op jit(solution)/shard_map/dot_general | solution.py:145
  83.5 0.9 fusion.9
  84.4 3.5 %convolution_convert_fusion = bf16[256,2304]{1,0:T(8,128)(2,1)S(1)} fusion(bf16[256,768]{0,1:T(8,128)(2,1)} %fusion.9, bf16[768,2304]{1,0:T(8,128)(2,1)} %all-gather.4.cloned.1.call-done), kind=kOutput, calls=%fused_computation.3 | convolution fusion | flops 906559488 | bytes 5111808 | tf_op jit(solution)/shard_map/dot_general | solution.py:60
  87.9 0.8 fusion.28
  88.8 0.9 copy.128
  89.7 1.2 copy.127
  90.8 2.0 pad_maximum_fusion
  94.4 0.9 copy.123
  95.3 1.9 copy.165
  97.2 87.1 %all-reduce.3.cloned.1.call-done = f32[2048,384]{0,1:T(8,128)} async-done(((f32[2048,384]{0,1:T(8,128)}), f32[2048,384]{0,1:T(8,128)}) %all-reduce.3.cloned.1.call-update) | async-done | bytes 3145744 | tf_op jit(solution)/shard_map/psum | solution.py:148
  184.4 3.5 %copy.166 = f32[2048,384]{1,0:T(8,128)} copy(f32[2048,384]{0,1:T(8,128)} %all-reduce.3.cloned.1.call-done) | data formatting | bytes 6291456
  188.1 1.6 reshape_reshape.3
  189.7 2.4 select_reduce_fusion
  192.1 2.8 %fusion.1 = f32[12,256,64]{1,2,0:T(8,128)S(1)} fusion(bf16[256,12,64]{0,2,1:T(8,128)(2,1)} %bitcast.181, f32[12,256,256]{1,2,0:T(8,128)} %get-tuple-element.69, f32[12,256]{1,0:T(8,128)S(1)} %get-tuple-element.68, pred[256]{0:T(512)(128)(4,1)S(1)} %add_compare_fusion.2), kind=kOutput, calls=%fused_computation.8 | convolution fusion | flops 103022592 | bytes 4337920 | tf_op jit(solution)/shard_map/hqk,khd->hqd/dot_general | solution.py:78
  195.3 0.7 fusion
  195.9 1.7 copy.130
  197.6 2.5 fusion.27
  200.7 2.6 fusion.29
  203.3 3.4 %slice_reduce_fusion.12 = (f32[64]{0:T(128)S(1)}, f32[64]{0:T(128)S(1)}, f32[64]{0:T(128)S(1)}, f32[64]{0:T(128)}, f32[64]{0:T(128)}, /*index=5*/f32[64]{0:T(128...) fusion(f32[12,64,4]{0,2,1:T(4,128)S(1)} %bitcast.175), kind=kLoop, calls=%fused_computation.72 | loop fusion | bytes 6144 | tf_op jit(solution)/shard_map/slice | solution.py:19
  206.8 3.4 %slice_reduce_fusion = (f32[64]{0:T(128)}, f32[64]{0:T(128)}, f32[64]{0:T(128)}, f32[64]{0:T(128)}, f32[64]{0:T(128)}, /*index=5*/f32[64]{0:T(128)}, f32[64]{0:T...) fusion(f32[12,64,4]{0,2,1:T(4,128)S(1)} %bitcast.176), kind=kLoop, calls=%fused_computation.60 | loop fusion | bytes 6144 | tf_op jit(solution)/shard_map/slice | solution.py:19
  210.1 1.4 constant_dynamic-update-slice_fusion.10
  211.5 1.4 constant_dynamic-update-slice_fusion.9
  212.9 1.4 constant_dynamic-update-slice_fusion.8
  214.3 1.4 constant_dynamic-update-slice_fusion.7
  215.6 1.4 constant_dynamic-update-slice_fusion.6
  217.0 1.4 constant_dynamic-update-slice_fusion.5
  218.4 1.4 constant_dynamic-update-slice_fusion.4
  219.8 1.4 constant_dynamic-update-slice_fusion.3
  221.1 1.4 constant_dynamic-update-slice_fusion.2
  222.5 0.8 constant_dynamic-update-slice_fusion.22
  223.3 0.8 constant_dynamic-update-slice_fusion.21
  224.0 0.8 constant_dynamic-update-slice_fusion.20
  224.8 0.8 constant_dynamic-update-slice_fusion.19
  226.2 1.3 stack.73
  227.6 1.4 stack.87
  229.7 2.6 copy.156
  232.3 17.9 %gather_fusion = bf16[1536,128]{1,0:T(8,128)(2,1)S(1)} fusion(bf16[512,12,128]{2,0,1:T(8,128)(2,1)} %copy.156, s32[1536]{0:T(1024)S(1)} %fusion.21), kind=kCustom, calls=%fused_computation | custom fusion | bytes 798720 | tf_op jit(solution)/shard_map/gather | solution.py:101
  251.0 1.4 convolution_add_fusion
  252.5 1.5 broadcast_in_dim.146
  253.9 2.8 %copy.159 = f32[12,256,64]{1,2,0:T(8,128)} copy(f32[12,256,64]{2,1,0:T(8,128)} %bitcast.168) | data formatting | bytes 1572864 | tf_op jit(solution)/shard_map/jit(_where)/broadcast_in_dim | solution.py:30
  256.9 1.4 select_convert_fusion
  258.3 2.5 fusion.6
  (60 shorter events, 6.0 us)
Async XLA Ops:
  7.2 10.7 %copy-start = (bf16[512,2048]{1,0:T(8,128)(2,1)S(1)}, bf16[512,2048]{1,0:T(8,128)(2,1)}, u32[]{:S(2)}) copy-start(bf16[512,2048]{1,0:T(8,128)(2,1)} %param.8) | copy-start | bytes 6291460
  7.2 77.3 %all-gather.4.cloned.1.call-start = ((), (), s32[]{:S(2)}) async-start(), calls=%async_computation.5 | async-start | bytes 3760128 | tf_op jit(solution)/shard_map/all_gather | solution.py:61
  10.5 13.7 %all-to-all-start = ((s32[16,32,1]{1,2,0:T(1,128)}), s32[16,32,1]{1,2,0:T(1,128)S(1)}, u32[]{:S(2)}, u32[]{:S(2)}) async-start(s32[16,32,1]{1,2,0:T(1,128)} %all_to_all.50), calls=%async_computation | async-start | bytes 16384 | tf_op jit(solution)/shard_map/all_to_all | solution.py:48
  17.9 9.9 %copy-start.2 = (bf16[1,256,768]{2,1,0:T(8,128)(2,1)S(1)}, bf16[1,256,768]{2,1,0:T(8,128)(2,1)}, u32[]{:S(2)}) copy-start(bf16[1,256,768]{2,1,0:T(8,128)(2,1)} %param.12) | copy-start | bytes 1179652
  24.2 17.3 %all-to-all-start.1 = ((bf16[16,32,384]{2,1,0:T(8,128)(2,1)}), bf16[16,32,384]{2,1,0:T(8,128)(2,1)S(1)}, u32[]{:S(2)}, u32[]{:S(2)}) async-start(bf16[16,32,384]{2,1,0:T(8,128)(2,1)} %bitcast.1), calls=%async_computation.1 | async-start | bytes 786432 | tf_op jit(solution)/shard_map/all_to_all | solution.py:47
  41.5 0.7 copy-start.3
  42.2 10.3 %all-to-all-start.3 = ((bf16[256,2,384]{2,0,1:T(8,128)(2,1)}), bf16[256,2,384]{2,0,1:T(8,128)(2,1)S(1)}, u32[]{:S(2)}, u32[]{:S(2)}) async-start(bf16[256,2,384]{2,0,1:T(8,128)(2,1)} %copy.164), calls=%async_computation.3 | async-start | bytes 786432 | tf_op jit(solution)/shard_map/all_to_all | solution.py:137
  52.6 9.6 %all-to-all-start.2 = ((bf16[2,256,384]{2,1,0:T(8,128)(2,1)}), bf16[2,256,384]{2,1,0:T(8,128)(2,1)S(1)}, u32[]{:S(2)}, u32[]{:S(2)}) async-start(bf16[2,256,384]{2,1,0:T(8,128)(2,1)} %bitcast.3), calls=%async_computation.2 | async-start | bytes 786432 | tf_op jit(solution)/shard_map/all_to_all | solution.py:54
  62.1 17.0 %all-to-all-start.4 = ((bf16[16,32,384]{2,1,0:T(8,128)(2,1)}), bf16[16,32,384]{2,1,0:T(8,128)(2,1)}, u32[]{:S(2)}, u32[]{:S(2)}) async-start(bf16[16,32,384]{2,1,0:T(8,128)(2,1)} %bitcast.50), calls=%async_computation.4 | async-start | bytes 786432 | tf_op jit(solution)/shard_map/all_to_all | solution.py:144
  66.9 117.5 %all-reduce.3.cloned.1.call-start = ((), (), s32[]{:S(2)}) async-start(), calls=%async_computation.8 | async-start | bytes 6291456 | tf_op jit(solution)/shard_map/psum | solution.py:148
  82.8 0.7 copy-start.4
  82.9 146.8 %all-gather.6.cloned.1.call-start = ((), (), s32[]{:S(2)}) async-start(), calls=%async_computation.6 | async-start | bytes 2359296 | tf_op jit(solution)/shard_map/all_gather | solution.py:90
  92.8 165.5 %all-gather.8.cloned.1.call-start = ((), (), s32[]{:S(2)}) async-start(), calls=%async_computation.7 | async-start | bytes 1253376 | tf_op jit(solution)/shard_map/all_gather | solution.py:134
  192.1 3.1 %copy-start.1 = (f32[12,256,256]{1,2,0:T(8,128)S(1)}, f32[12,256,256]{1,2,0:T(8,128)}, u32[]{:S(2)}) copy-start(f32[12,256,256]{1,2,0:T(8,128)} %get-tuple-element.69) | copy-start | bytes 9437188
Sparse Core Ops, SparseCore 0:
  10.3 52.3 all-gather.3
  83.0 101.3 all-reduce.2
  185.9 26.3 all-gather.5
  214.4 38.3 all-gather.7
where the time goes:
time: 269 us; the launch traced here: 267 us
  waiting for transfers between devices  120 us (45%)
  local copies, waits for them, and re-layouts  81 us (30%)
  starting transfers between devices  23 us (9%)
  matrix products  20.2 us (8%)
  between operations  14.7 us (5%)
  other arithmetic  8.78 us (3%)
    psum x1, waiting for transfers between devices, local(): proj_grad = lax.psum(grad_part, 'dp')  87.1 us
    unnamed x35, local copies, waits for them, and re-layouts  24 us
    gather x1, local copies, waits for them, and re-layouts, local(): chosen = shaped[safe_index, head_index, :]  17.9 us
    all_to_all x1, waiting for transfers between devices, local(): lax.all_to_all(emb_part, 'dp', split_axis=0, concat_axis=0, tiled=True)  12.1 us
    all_to_all x1, waiting for transfers between devices, local(): lax.all_to_all(picked_grad, 'dp', split_axis=0, concat_axis=0, tiled=True)  9.87 us
    slice x3, local copies, waits for them, and re-layouts, selection_shift(): shaped[head_number, :, head_number % dilation]  9.23 us
    all_to_all x1, starting transfers between devices, local(): lax.all_to_all(positions, 'dp', split_axis=0, concat_axis=0, tiled=True)  7.39 us
  transfers between devices with their start and end apart: 9, of which 6 were waited for; matrix products, arithmetic and copies ran while one was open for 39% of the time, Pallas kernels for 0%

commit v1 on v0

--- a/solution.py
+++ b/solution.py
@@ -145,7 +145,7 @@
     grad_part = lax.dot_general(
         tile_feats, slot_grad, (((0,), (0,)), ((), ())), preferred_element_type=jnp.float32
     )
-    proj_grad = lax.psum(grad_part, "dp")
+    proj_grad = jnp.sum(lax.all_gather(grad_part, "dp"), axis=0)
     return (local_emb[None], attn_branch[None], proj_grad)
 
 

time: 269 us -> 465 us (1.73)
  waiting for transfers between devices: 120 us -> 271 us
  blocking collectives: 0 us -> 25.2 us
  other arithmetic: 8.78 us -> 29.4 us
  local copies, waits for them, and re-layouts: 81 us -> 89.5 us
  starting transfers between devices: 23 us -> 15.4 us
    all_gather x0 -> x1, waiting for transfers between devices: none -> 238 us  [local(): proj_grad = jnp.sum(lax.all_gather(grad_part, 'dp'), axis=0)]
    psum x1 -> x0, waiting for transfers between devices: 87.1 us -> none  [local(): proj_grad = lax.psum(grad_part, 'dp')]
    unnamed x35 -> x38, local copies, waits for them, and re-layouts: 24 us -> 51 us
    all_to_all x0 -> x2, blocking collectives: none -> 25.2 us  [the longest x1 15.9 us: local(): lax.all_to_all(picked_grad, 'dp', split_axis=0, concat_axis=0, tiled=True)]
    reduce_sum x0 -> x1, other arithmetic: none -> 18.3 us  [local(): proj_grad = jnp.sum(lax.all_gather(grad_part, 'dp'), axis=0)]
    all_to_all x2 -> x0, waiting for transfers between devices: 13.3 us -> none  [the longest x1 9.87 us: local(): lax.all_to_all(picked_grad, 'dp', split_axis=0, concat_axis=0, tiled=True)]
    gather x1, local copies, waits for them, and re-layouts: 17.9 us -> 8.29 us  [local(): chosen = shaped[safe_index, head_index, :]]
    all_to_all x1, waiting for transfers between devices: 3.18 us -> 11.9 us  [local(): lax.all_to_all(emb_grad.reshape(nearby_length, D), 'seq', split_axis=1, c...]
  transfers between devices with their start and end apart: 9 -> 7, of which waited for: 6 -> 5; matrix products, arithmetic and copies ran while one was open for 39% -> 13% of each run, Pallas kernels for 0% -> 0%
where the time goes in v1:
time: 465 us; the launch traced here: 464 us
  waiting for transfers between devices  271 us (58%)
  local copies, waits for them, and re-layouts  89.5 us (19%)
  other arithmetic  29.4 us (6%)
  blocking collectives  25.2 us (5%)
  matrix products  17.8 us (4%)
  starting transfers between devices  15.4 us (3%)
  between operations  14.9 us (3%)
    all_gather x1, waiting for transfers between devices, local(): proj_grad = jnp.sum(lax.all_gather(grad_part, 'dp'), axis=0)  238 us
    unnamed x38, local copies, waits for them, and re-layouts  51 us
    reduce_sum x1, other arithmetic, local(): proj_grad = jnp.sum(lax.all_gather(grad_part, 'dp'), axis=0)  18.3 us
    all_to_all x1, blocking collectives, local(): lax.all_to_all(picked_grad, 'dp', split_axis=0, concat_axis=0, tiled=True)  15.9 us
    all_to_all x1, waiting for transfers between devices, local(): lax.all_to_all(emb_part, 'dp', split_axis=0, concat_axis=0, tiled=True)  12.9 us
    all_to_all x1, waiting for transfers between devices, local(): lax.all_to_all(emb_grad.reshape(nearby_length, D), 'seq', split_axis=1, c...  11.9 us
    all_to_all x1, blocking collectives, local(): lax.all_to_all(slide_rows, 'seq', split_axis=0, concat_axis=1, tiled=True)  9.31 us
  transfers between devices with their start and end apart: 7, of which 5 were waited for; matrix products, arithmetic and copies ran while one was open for 13% of the time, Pallas kernels for 0%

profile of v1, /device:TPU:0, one launch (start us, length us, event | category | flops | bytes accessed | tf_op | source)
XLA Modules:
  0.0 463.7 jit_solution(7182529851629736067)
XLA Ops:
  7.2 0.7 all-gather.6.cloned.1.call-update
  7.9 0.5 broadcast.341
  8.4 1.3 reduce.56
  9.8 0.7 all_to_all.50
  10.5 7.4 %all-to-all-start = ((s32[16,32,1]{1,2,0:T(1,128)}), s32[16,32,1]{1,2,0:T(1,128)S(1)}, u32[]{:S(2)}, u32[]{:S(2)}) async-start(s32[16,32,1]{1,2,0:T(1,128)} %all_to_all.50), calls=%async_computation | async-start | bytes 16384 | tf_op jit(solution)/shard_map/all_to_all | solution.py:48
  17.9 3.4 convolution_convert_fusion.2
  21.3 2.9 all-to-all-done
  24.2 3.7 all-to-all-start.1
  27.9 0.7 reduce.57
  28.6 0.1 all_to_all.52
  28.7 12.9 %all-to-all-done.1 = bf16[16,32,384]{2,1,0:T(8,128)(2,1)S(1)} async-done(((bf16[16,32,384]{2,1,0:T(8,128)(2,1)}), bf16[16,32,384]{2,1,0:T(8,128)(2,1)S(1)}, u32[]{:S(2)}, u32[]{:S(2)}) %all-to-all-start.1) | async-done | bytes 393248 | tf_op jit(solution)/shard_map/all_to_all | solution.py:47
  41.6 2.4 scatter_custom_fusion
  44.1 9.3 %all_to_all.71 = bf16[2,256,384]{2,1,0:T(8,128)(2,1)S(1)} all-to-all(bf16[2,256,384]{2,1,0:T(8,128)(2,1)S(1)} %bitcast.187), channel_id=1, replica_groups=mesh['dp'=16,'seq'=2] {'seq'}, dimensions={0} | all-to-all | bytes 786432 | tf_op jit(solution)/shard_map/all_to_all | solution.py:54
  53.4 0.9 bitcast_convert_fusion
  54.3 2.3 copy.122
  56.7 0.1 convert_reduce_fusion
  56.8 0.2 multiply_reduce_fusion
  57.1 1.3 fusion.9
  58.4 4.3 all-gather.6.cloned.1.call-done
  62.7 3.1 convolution_convert_fusion
  65.8 0.8 fusion.28
  66.6 0.9 copy.125
  67.6 1.2 copy.124
  68.7 2.1 pad_maximum_fusion
  70.9 0.7 all-gather.10.cloned.1.call-update
  71.6 1.8 all_to_all.59
  73.4 1.8 copy.161
  75.2 4.2 all-to-all-start.3
  79.4 11.9 %all-to-all-done.3 = bf16[256,2,384]{2,0,1:T(8,128)(2,1)} async-done(((bf16[256,2,384]{2,0,1:T(8,128)(2,1)}), bf16[256,2,384]{2,0,1:T(8,128)(2,1)}, u32[]{:S(2)}, u32[]{:S(2)}) %all-to-all-start.3) | async-done | bytes 393248 | tf_op jit(solution)/shard_map/all_to_all | solution.py:137
  91.4 1.0 concatenate.30
  92.4 2.6 gather_fusion.1
  95.0 15.9 %all_to_all.72 = bf16[16,32,384]{2,1,0:T(8,128)(2,1)S(1)} all-to-all(bf16[16,32,384]{2,1,0:T(8,128)(2,1)} %bitcast.186), channel_id=1, replica_groups=mesh['dp'=16,'seq'=2] {'dp'}, dimensions={0} | all-to-all | bytes 786432 | tf_op jit(solution)/shard_map/all_to_all | solution.py:144
  110.9 2.6 convolution_bitcast_fusion
  114.3 0.1 copy.121
  114.5 0.1 fusion.21
  114.6 0.2 copy.120
  114.8 0.9 copy.162
  115.7 0.2 copy.123
  115.9 1.6 reshape_reshape.3
  117.5 2.4 select_reduce_fusion
  119.9 0.1 copy.140
  120.0 2.6 fusion
  122.6 0.1 copy.157
  122.7 2.5 fusion.1
  125.2 0.5 copy.127
  125.7 2.8 slice_reduce_fusion.12
  128.5 2.8 slice_reduce_fusion
  131.4 0.4 fusion.27
  132.0 2.0 fusion.29
  134.2 1.9 copy.153
  136.1 8.3 %gather_fusion = bf16[1536,128]{1,0:T(8,128)(2,1)S(1)} fusion(bf16[512,12,128]{2,0,1:T(8,128)(2,1)S(1)} %copy.153, s32[1536]{0:T(1024)S(1)} %fusion.21), kind=kCustom, calls=%fused_computation | custom fusion | bytes 798720 | tf_op jit(solution)/shard_map/gather | solution.py:101
  144.4 0.5 select_reduce_fusion.1
  144.8 0.3 fusion.12
  145.2 0.1 copy.158
  145.3 0.1 copy.160
  145.4 0.4 convolution_add_fusion
  145.8 0.3 broadcast_in_dim.146
  146.1 1.3 copy.156
  147.5 1.3 select_convert_fusion
  148.8 2.9 fusion.6
  151.6 237.9 %all-gather.12.cloned.1.call-done = f32[32768,384]{0,1:T(8,128)} async-done(((f32[2048,384]{0,1:T(8,128)}), f32[32768,384]{0,1:T(8,128)}) %all-gather.12.cloned.1.call-update) | async-done | bytes 50331664 | tf_op jit(solution)/shard_map/all_gather | solution.py:148
  389.5 45.8 %copy.191 = f32[48,8,16,2048]{3,2,1,0:T(8,128)} copy(f32[48,8,16,2048]{3,1,2,0:T(8,128)} %bitcast.173) | data formatting | bytes 100663296
  435.3 18.3 %bitcast_reduce_fusion = f32[2048,384]{0,1:T(8,128)} fusion(f32[48,8,16,2048]{3,2,1,0:T(8,128)} %copy.191), kind=kLoop, calls=%fused_computation.3 | loop fusion | flops 11796480 | bytes 53477376 | tf_op jit(solution)/shard_map/reduce_sum | solution.py:148
  453.7 3.5 copy.163
  (62 shorter events, 0.8 us)
Async XLA Ops:
  7.2 10.7 %copy-start = (bf16[512,2048]{1,0:T(8,128)(2,1)S(1)}, bf16[512,2048]{1,0:T(8,128)(2,1)}, u32[]{:S(2)}) copy-start(bf16[512,2048]{1,0:T(8,128)(2,1)} %param.8) | copy-start | bytes 6291460
  7.2 55.5 %all-gather.6.cloned.1.call-start = ((), (), s32[]{:S(2)}) async-start(), calls=%async_computation.5 | async-start | bytes 3760128 | tf_op jit(solution)/shard_map/all_gather | solution.py:61
  10.5 13.7 %all-to-all-start = ((s32[16,32,1]{1,2,0:T(1,128)}), s32[16,32,1]{1,2,0:T(1,128)S(1)}, u32[]{:S(2)}, u32[]{:S(2)}) async-start(s32[16,32,1]{1,2,0:T(1,128)} %all_to_all.50), calls=%async_computation | async-start | bytes 16384 | tf_op jit(solution)/shard_map/all_to_all | solution.py:48
  24.2 32.9 %copy-start.5 = (f32[768]{0:T(1024)S(1)}, f32[768]{0:T(1024)}, u32[]{:S(2)}) copy-start(f32[768]{0:T(1024)} %param.13) | copy-start | bytes 9220
  24.2 17.4 %all-to-all-start.1 = ((bf16[16,32,384]{2,1,0:T(8,128)(2,1)}), bf16[16,32,384]{2,1,0:T(8,128)(2,1)S(1)}, u32[]{:S(2)}, u32[]{:S(2)}) async-start(bf16[16,32,384]{2,1,0:T(8,128)(2,1)} %bitcast.1), calls=%async_computation.1 | async-start | bytes 786432 | tf_op jit(solution)/shard_map/all_to_all | solution.py:47
  27.9 106.3 %all-gather.8.cloned.1.call-start = ((), (), s32[]{:S(2)}) async-start(), calls=%async_computation.6 | async-start | bytes 2359296 | tf_op jit(solution)/shard_map/all_gather | solution.py:90
  68.7 22.6 %copy-start.2 = (bf16[256,768]{0,1:T(8,128)(2,1)}, bf16[256,768]{0,1:T(8,128)(2,1)S(1)}, u32[]{:S(2)}) copy-start(bf16[256,768]{0,1:T(8,128)(2,1)S(1)} %copy.124) | copy-start | bytes 1179652
  70.8 77.9 %all-gather.10.cloned.1.call-start = ((), (), s32[]{:S(2)}) async-start(), calls=%async_computation.7 | async-start | bytes 1253376 | tf_op jit(solution)/shard_map/all_gather | solution.py:134
  75.2 16.2 %all-to-all-start.3 = ((bf16[256,2,384]{2,0,1:T(8,128)(2,1)}), bf16[256,2,384]{2,0,1:T(8,128)(2,1)}, u32[]{:S(2)}, u32[]{:S(2)}) async-start(bf16[256,2,384]{2,0,1:T(8,128)(2,1)} %copy.161), calls=%async_computation.3 | async-start | bytes 786432 | tf_op jit(solution)/shard_map/all_to_all | solution.py:137
  79.4 310.2 %all-gather.12.cloned.1.call-start = ((), (), s32[]{:S(2)}) async-start(), calls=%async_computation.8 | async-start | bytes 53477376 | tf_op jit(solution)/shard_map/all_gather | solution.py:148
  113.5 3.9 copy-start.3
  117.5 5.2 %copy-start.4 = (bf16[256,768]{0,1:T(8,128)(2,1)S(1)}, bf16[256,768]{0,1:T(8,128)(2,1)}, u32[]{:S(2)}) copy-start(bf16[256,768]{0,1:T(8,128)(2,1)} %copy.125) | copy-start | bytes 1179652
  435.3 21.9 %copy-start.1 = (bf16[512,2048]{1,0:T(8,128)(2,1)S(1)}, bf16[512,2048]{1,0:T(8,128)(2,1)}, u32[]{:S(2)}) copy-start(bf16[512,2048]{1,0:T(8,128)(2,1)} %param.8) | copy-start | bytes 6291460
Sparse Core Ops, SparseCore 0:
  10.3 52.3 all-gather.5
  70.9 30.3 all-gather.7
  103.7 38.3 all-gather.9
  143.4 246.0 all-gather.11
